TPU v7x, 32 devices: a whole 2x2x4 slice. The times are simulated.
32 devices in a mesh: req: 8 (over z, x), tp: 4 (over y, core).
Axes of the slice: x: 2, y: 2, z: 4, core: 2. Of those that a mesh axis runs over, the one named last changes fastest.
Arguments:
- hidden: bfloat16 [2048, 2048], P('req'), may hold values from -10.5 to 10.5
- lengths: int32 [8], replicated, may hold values from 1 to 1024, 2048 in all
- dealing: int32 [8], replicated, may hold values from 0 to 7, each once
- norm_gain: bfloat16 [2048], replicated, may hold values from 0.5 to 1.5
- w_query: bfloat16 [2048, 2048], P(None, 'tp'), may hold values from -0.125 to 0.125
- w_key: bfloat16 [2048, 1024], P(None, 'tp'), may hold values from -0.125 to 0.125
- w_value: bfloat16 [2048, 1024], P(None, 'tp'), may hold values from -0.125 to 0.125
- query_gain: bfloat16 [128], replicated, may hold values from 0.5 to 8
- key_gain: bfloat16 [128], replicated, may hold values from 0.5 to 8
- w_out: bfloat16 [2048, 2048], P(None, 'tp'), may hold values from -0.125 to 0.125
Outputs:
- hidden_out: bfloat16 [2048, 2048], P('req', 'tp')
- kv_cache: bfloat16 [2, 8, 1024, 1024], P(None, 'req', None, 'tp')
Inputs may be any that keep to these rules, and one draw needn't show every extreme that they name: The lengths sum to 2048; the largest is exactly 1024. A permutation: dealt slot j, on device j of req, holds prompt dealing[j].
All inputs are finite; a program needn't handle non-finite values.
Results may differ from a plain program's by a relative error of at most 0.012.
The roundings to bfloat16 on the way count: a program that leaves them out, or rounds other values in their place, can miss the bound.
Values may be sent and summed in bfloat16 or wider, within the bound.
A program may use at most 128 MiB of HBM per device.

v0:
```python
import jax
import jax.numpy as jnp
from jax import lax
from jax.sharding import PartitionSpec as P

EPS = 1e-06
THETA = 1000000.0


def rms_rows(values, scale_gain):
    inv_rms = lax.rsqrt(jnp.mean(values * values, axis=-1, keepdims=True) + EPS)
    return values * inv_rms * scale_gain


def rotate(values, positions):
    features = values.shape[-1]
    half_width = features // 2
    frequency = THETA ** (-(jnp.arange(half_width).astype(jnp.float32) * 2.0) / features)
    angles = positions.astype(jnp.float32)[:, None] * frequency[None, :]
    cosine = jnp.cos(angles)[:, None, :]
    sine_part = jnp.sin(angles)[:, None, :]
    first_half = values[..., :half_width]
    second_half = values[..., half_width:]
    return jnp.concatenate(
        [
            first_half * cosine - second_half * sine_part,
            second_half * cosine + first_half * sine_part,
        ],
        axis=-1,
    )


def project(normed, w_query, w_key, w_value, query_gain, key_gain, positions):
    head_dim = query_gain.shape[0]
    row_count = normed.shape[0]
    query_rows = jnp.dot(normed, w_query, preferred_element_type=jnp.float32).reshape(
        row_count, -1, head_dim
    )
    key_rows = jnp.dot(normed, w_key, preferred_element_type=jnp.float32).reshape(
        row_count, -1, head_dim
    )
    value_rows = jnp.dot(normed, w_value, preferred_element_type=jnp.float32).astype(jnp.bfloat16)
    query_rows = rotate(rms_rows(query_rows, query_gain.astype(jnp.float32)), positions).astype(
        jnp.bfloat16
    )
    key_rows = rotate(rms_rows(key_rows, key_gain.astype(jnp.float32)), positions).astype(
        jnp.bfloat16
    )
    return (query_rows.reshape(row_count, -1), key_rows.reshape(row_count, -1), value_rows)


def attend(query_slot, key_slot, value_slot, prompt_length, head_dim):
    slot_len, query_width = query_slot.shape
    kv_heads = key_slot.shape[1] // head_dim
    group_size = query_width // head_dim // kv_heads
    queries = query_slot.reshape(slot_len, kv_heads, group_size, head_dim)
    keys_split = key_slot.reshape(slot_len, kv_heads, head_dim)
    values_split = value_slot.reshape(slot_len, kv_heads, head_dim)
    scores = jnp.einsum(
        "qkgd,skd->kgqs", queries, keys_split, preferred_element_type=jnp.float32
    ) * head_dim ** (-0.5)
    offsets = jnp.arange(slot_len, dtype=jnp.int32)
    allowed = (offsets[None, :] <= offsets[:, None]) & (offsets[None, :] < prompt_length)
    scores = jnp.where(allowed[None, None], scores, -jnp.inf)
    row_max = jnp.max(scores, axis=-1, keepdims=True)
    weights = jnp.exp(scores - row_max)
    weights = (weights / jnp.sum(weights, axis=-1, keepdims=True)).astype(jnp.bfloat16)
    mixture = jnp.einsum(
        "kgqs,skd->qkgd", weights, values_split, preferred_element_type=jnp.float32
    )
    return mixture.astype(jnp.bfloat16).reshape(slot_len, query_width)


def on_device(
    hidden, lengths, dealing, norm_gain, w_query, w_key, w_value, query_gain, key_gain, w_out
):
    devices = lax.axis_size("req")
    home_index = lax.axis_index("req")
    slice_index = lax.axis_index("tp")
    tok_rows, features = hidden.shape
    head_dim = query_gain.shape[0]
    out_width = w_out.shape[1]
    slot_len = 4 * tok_rows
    capacity = slot_len // devices
    prompt_total = lengths.shape[0]
    prompt_ids = jnp.arange(prompt_total, dtype=jnp.int32)
    prompt_ends = jnp.cumsum(lengths)
    starts = prompt_ends - lengths
    packed_ids = jnp.arange(tok_rows, dtype=jnp.int32) * devices + home_index
    segment = jnp.sum((packed_ids[:, None] >= prompt_ends[None, :]).astype(jnp.int32), axis=1)
    seg_onehot = (segment[:, None] == prompt_ids[None, :]).astype(jnp.int32)
    positions = packed_ids - jnp.sum(seg_onehot * starts[None, :], axis=1)
    inverse = jnp.zeros((prompt_total,), jnp.int32).at[dealing].set(prompt_ids)
    deal_hot = (dealing[:, None] == prompt_ids[None, :]).astype(jnp.int32)
    dealt_starts = jnp.sum(deal_hot * starts[None, :], axis=1)
    dealt_lengths = jnp.sum(deal_hot * lengths[None, :], axis=1)
    first_offset = jnp.mod(home_index - dealt_starts, devices)
    ranks = jnp.arange(capacity, dtype=jnp.int32)
    slot_offset = first_offset[None, :] + ranks[:, None] * devices
    send_valid = slot_offset < dealt_lengths[None, :]
    send_rows = jnp.where(
        send_valid, (dealt_starts[None, :] + slot_offset - home_index) // devices, 0
    ).reshape(-1)
    my_start = lax.dynamic_index_in_dim(dealt_starts, home_index, 0, keepdims=False)
    my_length = lax.dynamic_index_in_dim(dealt_lengths, home_index, 0, keepdims=False)
    roll_shift = jnp.mod(my_start, devices)
    my_slots = jnp.sum(seg_onehot * inverse[None, :], axis=1)
    back_rows = positions // devices * devices + my_slots
    offsets = jnp.arange(slot_len, dtype=jnp.int32)
    gain_values = norm_gain.astype(jnp.float32)
    picked = jnp.take(hidden, send_rows, axis=0).reshape(capacity, devices, hidden.shape[1])
    arrived = lax.all_to_all(
        jnp.where(send_valid[:, :, None], picked, jnp.zeros((), hidden.dtype)),
        "req",
        split_axis=1,
        concat_axis=1,
        tiled=True,
    )
    slot_hidden = jnp.roll(arrived, -roll_shift, axis=1).reshape(slot_len, arrived.shape[2])
    normed = rms_rows(slot_hidden.astype(jnp.float32), gain_values).astype(jnp.bfloat16)
    query_slot, key_slot, value_slot = project(
        normed, w_query, w_key, w_value, query_gain, key_gain, offsets
    )
    mixture = attend(query_slot, key_slot, value_slot, my_length, head_dim)
    sendback = jnp.roll(mixture.reshape(capacity, devices, mixture.shape[1]), roll_shift, axis=1)
    returned = lax.all_to_all(sendback, "req", split_axis=1, concat_axis=1, tiled=True)
    attended = jnp.take(returned.reshape(capacity * devices, -1), back_rows, axis=0)
    kv_cache = jnp.stack([key_slot, value_slot])[:, None]
    summed = jnp.dot(
        lax.all_gather(attended, "tp", axis=1, tiled=True),
        w_out,
        preferred_element_type=jnp.float32,
    )
    branch = lax.optimization_barrier(summed.astype(jnp.bfloat16))
    residual = lax.dynamic_slice_in_dim(hidden, slice_index * out_width, out_width, 1)
    hidden_out = (residual.astype(jnp.float32) + branch.astype(jnp.float32)).astype(jnp.bfloat16)
    return (hidden_out, kv_cache)


def solution(mesh):
    in_specs = (
        P("req", None),
        P(),
        P(),
        P(),
        P(None, "tp"),
        P(None, "tp"),
        P(None, "tp"),
        P(),
        P(),
        P(None, "tp"),
    )
    out_specs = (P("req", "tp"), P(None, "req", None, "tp"))
    return jax.shard_map(
        on_device, mesh=mesh, in_specs=in_specs, out_specs=out_specs, check_vma=False
    )
```

profile of v0, /device:TPU:17, one launch (start us, length us, event | category | flops | bytes accessed | tf_op | source)
XLA Modules:
  0.0 244.5 jit_solution(12086319305798806099)
XLA Ops:
  7.2 0.0 copy-start
  7.2 1.0 reduce-window.8
  8.2 0.7 bitcast_subtract_fusion
  8.8 0.9 select_reduce_fusion.2
  9.7 0.7 compare_select_fusion.7
  10.4 0.1 fusion.39
  10.5 0.1 compare_and_fusion
  10.5 0.1 copy.72
  10.7 0.1 lt.124
  10.8 0.1 copy.73
  10.9 0.1 sub.93
  11.0 10.2 %gather_fusion = bf16[1024,2048]{1,0:T(8,128)(2,1)} fusion(bf16[256,2048]{1,0:T(8,128)(2,1)} %param.10, s32[1024]{0:T(1024)S(1)} %broadcast_clamp_fusion), kind=kCustom, calls=%fused_computation | custom fusion | bytes 8392704 | tf_op jit(solution)/shard_map/jit(_take)/gather | solution.py:111
  21.2 10.2 %fusion.16 = bf16[128,8,2048]{2,0,1:T(8,128)(2,1)} fusion(bf16[128,8,2048]{2,1,0:T(8,128)(2,1)} %bitcast.83, pred[128,8]{0,1:T(8,128)(4,1)S(1)} %get-tuple-element.20, pred[128,8]{0,1:T(8,128)(4,1)S(1)} %get-tuple-element.21), kind=kLoop, calls=%fused_computation.27 | loop fusion | flops 4194304 | bytes 8390656 | tf_op jit(solution)/shard_map/jit(_where)/select_n | solution.py:113
  31.4 5.7 %all-to-all-start = ((bf16[128,8,2048]{2,0,1:T(8,128)(2,1)}), bf16[128,8,2048]{2,0,1:T(8,128)(2,1)}, u32[]{:S(2)}, u32[]{:S(2)}) async-start(bf16[128,8,2048]{2,0,1:T(8,128)(2,1)} %fusion.16), calls=%async_computation | async-start | bytes 8388608 | tf_op jit(solution)/shard_map/all_to_all | solution.py:112
  37.1 0.6 dynamic_slice.19
  39.7 0.6 dynamic_slice.21
  40.3 0.0 copy-done.5
  40.3 4.0 %copy.93 = bf16[512,2048]{1,0:T(8,128)(2,1)} copy(bf16[512,2048]{0,1:T(8,128)(2,1)} %bitcast.87) | data formatting | bytes 4194304 | tf_op jit(solution)/shard_map/dot_general | solution.py:36
  44.3 0.0 copy-done.7
  44.3 0.0 copy-done.3
  44.3 1.4 copy.90
  45.7 0.0 copy-done.8
  45.7 0.7 iota_compare_fusion.2
  46.4 1.0 multiply_cosine_fusion
  47.4 1.3 fusion.19
  48.7 77.7 %all-to-all-done = bf16[128,8,2048]{2,0,1:T(8,128)(2,1)} async-done(((bf16[128,8,2048]{2,0,1:T(8,128)(2,1)}), bf16[128,8,2048]{2,0,1:T(8,128)(2,1)}, u32[]{:S(2)}, u32[]{:S(2)}) %all-to-all-start) | async-done | bytes 4194336 | tf_op jit(solution)/shard_map/all_to_all | solution.py:112
  126.5 4.5 %copy.75 = bf16[128,8,2048]{2,1,0:T(8,128)(2,1)S(1)} copy(bf16[128,8,2048]{2,0,1:T(8,128)(2,1)} %all-to-all-done) | data formatting | bytes 8388608 | tf_op jit(solution)/shard_map/all_to_all | solution.py:112
  130.9 5.2 %fusion.5 = (f32[128,8]{1,0:T(8,128)S(1)}, bf16[128,8,2048]{2,1,0:T(8,128)(2,1)}) fusion(s32[]{:T(128)S(6)} %select_n.166, bf16[128,8,2048]{2,1,0:T(8,128)(2,1)S(1)} %copy.75), kind=kLoop, calls=%fused_computation.14 | loop fusion | flops 14679040 | bytes 8392708 | tf_op jit(solution)/shard_map/reduce_sum | solution.py:11
  136.2 0.1 rsqrt.29
  136.3 5.3 %multiply_reduce_fusion = (f32[1024,4]{0,1:T(4,128)S(1)}, f32[1024,4,128]{0,2,1:T(8,128)S(1)}) fusion(bf16[4,128,2048]{2,1,0:T(8,128)(2,1)} %bitcast.88, bf16[128,8,2048]{2,1,0:T(8,128)(2,1)} %get-tuple-element.19, f32[2048]{0:T(1024)S(1)} %convert_element_type.122, f32[128,8]{1,0:T(8,128)S(1)} %add_rsqrt_fusion), kind=kOutput, calls=%fused_computation.37 | convolution fusion | flops 2156916736 | bytes 8417280 | tf_op jit(solution)/shard_map/dot_general | solution.py:36
  141.6 0.4 multiply_multiply_fusion
  142.1 1.2 subtract_convert_fusion
  143.2 2.4 copy.80
  145.6 1.4 copy.79
  147.0 4.0 %multiply_reduce_fusion.1 = (f32[1024,2]{0,1:T(2,128)S(1)}, f32[1024,2,128]{0,2,1:T(8,128)S(1)}) fusion(bf16[2,128,2048]{2,1,0:T(8,128)(2,1)} %bitcast.91, bf16[128,8,2048]{2,1,0:T(8,128)(2,1)} %get-tuple-element.19, f32[2048]{0:T(1024)S(1)} %convert_element_type.122, f32[128,8]{1,0:T(8,128)S(1)} %add_rsqrt_fusion), kind=kOutput, calls=%fused_computation.51 | convolution fusion | flops 1082652672 | bytes 6311936 | tf_op jit(solution)/shard_map/dot_general | solution.py:39
  151.0 0.0 copy-start.1
  151.0 0.2 multiply_multiply_fusion.1
  151.2 0.9 multiply_subtract_fusion
  152.1 0.0 copy-done.6
  152.1 1.2 copy-done.1
  153.3 2.3 fusion.28
  155.6 0.0 copy-done.4
  155.6 11.5 %fusion.53 = (f32[2,2,1024]{2,1,0:T(2,128)S(1)}, f32[2,2,1024,1024]{2,3,1,0:T(8,128)}) fusion(pred[1024,1024]{0,1:T(8,128)(4,1)S(1)} %copy-done.2, bf16[1024,2,2,64]{3,0,2,1:T(8,128)(2,1)} %copy.80, bf16[1024,2,2,64]{3,0,2,1:T(8,128)(2,1)} %copy.79, bf16[1024,2,64]{0,2,1:T(8,128)(2,1)} %get-tuple-element.25, bf16[1024,2,64]{0,2,1:T(8,128)(2,1)S(1)} %get-tuple-element.24), kind=kOutput, calls=%fused_computation.119 | convolution fusion | flops 1093665792 | bytes 19415040 | tf_op jit(solution)/shard_map/sub | solution.py:66
  167.1 7.2 %fusion.27 = bf16[1024,2,2,128]{0,3,2,1:T(8,128)(2,1)S(1)} fusion(bf16[1024,2,128,1]{0,2,3,1:T(8,128)(2,1)} %bitcast.92, f32[2,2,1024,1024]{2,3,1,0:T(8,128)} %get-tuple-element.33, f32[2,2,1024]{2,1,0:T(2,128)S(1)} %get-tuple-element.32), kind=kOutput, calls=%fused_computation.40 | convolution fusion | flops 1082654720 | bytes 18366464 | tf_op jit(solution)/shard_map/kgqs,skd->qkgd/dot_general | solution.py:68
  174.3 2.0 copy.83
  176.4 1.7 reshape_reshape.4
  178.1 0.7 fusion.31
  178.8 1.3 copy.84
  180.1 7.8 %all-to-all-start.1 = ((bf16[128,8,512]{2,0,1:T(8,128)(2,1)}), bf16[128,8,512]{2,0,1:T(8,128)(2,1)}, u32[]{:S(2)}, u32[]{:S(2)}) async-start(bf16[128,8,512]{2,0,1:T(8,128)(2,1)} %copy.84), calls=%async_computation.1 | async-start | bytes 2097152 | tf_op jit(solution)/shard_map/all_to_all | solution.py:126
  187.9 0.0 all-gather.2.cloned.1.call-start
  187.9 0.6 scatter_custom_fusion
  188.5 0.1 convert_reduce_fusion
  188.6 0.1 select_reduce_fusion.1
  188.8 21.4 %all-to-all-done.1 = bf16[128,8,512]{2,0,1:T(8,128)(2,1)} async-done(((bf16[128,8,512]{2,0,1:T(8,128)(2,1)}), bf16[128,8,512]{2,0,1:T(8,128)(2,1)}, u32[]{:S(2)}, u32[]{:S(2)}) %all-to-all-start.1) | async-done | bytes 1048608 | tf_op jit(solution)/shard_map/all_to_all | solution.py:126
  210.2 1.8 copy.98
  212.0 1.2 gather_fusion.1
  213.2 0.8 broadcast_select_fusion
  214.0 0.0 all-gather.2.cloned.1.call-update
  214.0 1.1 maximum_convert_fusion
  215.1 1.1 maximum_bitcast_fusion
  216.2 1.3 copy.86
  217.5 16.4 %all-gather.2.cloned.1.call-done = bf16[256,2048]{1,0:T(8,128)(2,1)} async-done(((bf16[256,512]{1,0:T(8,128)(2,1)}), bf16[256,2048]{1,0:T(8,128)(2,1)}) %all-gather.2.cloned.1.call-update) | async-done | bytes 1048592 | tf_op jit(solution)/shard_map/all_gather | solution.py:130
  233.9 1.9 convolution_convert_fusion
  235.9 1.7 add_convert_fusion.1
  (25 shorter events, 0.2 us)
Async XLA Ops:
  7.2 226.8 %copy-start = (bf16[2048,512]{1,0:T(8,128)(2,1)S(1)}, bf16[2048,512]{1,0:T(8,128)(2,1)}, u32[]{:S(2)}) copy-start(bf16[2048,512]{1,0:T(8,128)(2,1)} %param.19) | copy-start | bytes 6291460
  31.4 8.9 %copy-start.5 = (bf16[2048]{0:T(1024)(128)(2,1)S(1)}, bf16[2048]{0:T(1024)(128)(2,1)}, u32[]{:S(2)}) copy-start(bf16[2048]{0:T(1024)(128)(2,1)} %param.13) | copy-start | bytes 12292
  31.4 95.0 %all-to-all-start = ((bf16[128,8,2048]{2,0,1:T(8,128)(2,1)}), bf16[128,8,2048]{2,0,1:T(8,128)(2,1)}, u32[]{:S(2)}, u32[]{:S(2)}) async-start(bf16[128,8,2048]{2,0,1:T(8,128)(2,1)} %fusion.16), calls=%async_computation | async-start | bytes 8388608 | tf_op jit(solution)/shard_map/all_to_all | solution.py:112
  37.1 7.2 %copy-start.7 = (bf16[128]{0:T(256)(128)(2,1)S(1)}, bf16[128]{0:T(256)(128)(2,1)}, u32[]{:S(2)}) copy-start(bf16[128]{0:T(256)(128)(2,1)} %param.17) | copy-start | bytes 772
  37.1 7.2 %copy-start.3 = (bf16[2048,256]{1,0:T(8,128)(2,1)S(1)}, bf16[2048,256]{1,0:T(8,128)(2,1)}, u32[]{:S(2)}) copy-start(bf16[2048,256]{1,0:T(8,128)(2,1)} %param.15) | copy-start | bytes 3145732
  37.1 8.6 %copy-start.8 = (bf16[128]{0:T(256)(128)(2,1)S(1)}, bf16[128]{0:T(256)(128)(2,1)}, u32[]{:S(2)}) copy-start(bf16[128]{0:T(256)(128)(2,1)} %param.18) | copy-start | bytes 772
  147.0 5.1 %copy-start.6 = (bf16[2048,256]{1,0:T(8,128)(2,1)S(1)}, bf16[2048,256]{1,0:T(8,128)(2,1)}, u32[]{:S(2)}) copy-start(bf16[2048,256]{1,0:T(8,128)(2,1)} %param.16) | copy-start | bytes 3145732
  151.0 2.3 copy-start.1
  153.3 2.3 copy-start.4
  153.3 2.3 copy-start.2
  180.1 30.1 %all-to-all-start.1 = ((bf16[128,8,512]{2,0,1:T(8,128)(2,1)}), bf16[128,8,512]{2,0,1:T(8,128)(2,1)}, u32[]{:S(2)}, u32[]{:S(2)}) async-start(bf16[128,8,512]{2,0,1:T(8,128)(2,1)} %copy.84), calls=%async_computation.1 | async-start | bytes 2097152 | tf_op jit(solution)/shard_map/all_to_all | solution.py:126
  187.9 46.0 %all-gather.2.cloned.1.call-start = ((), (), s32[]{:S(2)}) async-start(), calls=%async_computation.2 | async-start | bytes 1310720 | tf_op jit(solution)/shard_map/all_gather | solution.py:130
Sparse Core Ops, SparseCore 0:
  214.1 19.7 all-gather.1
where the time goes:
time: 247 us; the launch traced here: 244 us
  waiting for transfers between devices  116 us (47%)
  local copies, waits for them, and re-layouts  36.7 us (15%)
  matrix products  32.3 us (13%)
  other arithmetic  30.2 us (12%)
  between operations  16.2 us (7%)
  starting transfers between devices  13.5 us (5%)
    all_to_all x1, waiting for transfers between devices, on_device(): lax.all_to_all(jnp.where(send_valid[:, :, None], picked, jnp.zeros((), hi...  77.7 us
    all_to_all x1, waiting for transfers between devices, on_device(): lax.all_to_all(sendback, 'req', split_axis=1, concat_axis=1, tiled=True)  21.4 us
    all_gather x1, waiting for transfers between devices, on_device(): lax.all_gather(attended, 'tp', axis=1, tiled=True)  16.4 us
    sub x1, matrix products, attend(): weights = jnp.exp(scores - row_max)  11.5 us
    gather x1, local copies, waits for them, and re-layouts, on_device(): jnp.take(hidden, send_rows, axis=0)  10.2 us
    select_n x1, other arithmetic, on_device(): jnp.where(send_valid[:, :, None], picked, jnp.zeros((), hidden.dtype))  10.2 us
    all_to_all x1, starting transfers between devices, on_device(): lax.all_to_all(sendback, 'req', split_axis=1, concat_axis=1, tiled=True)  7.78 us
    dot_general x1, matrix products, attend(): jnp.einsum('kgqs,skd->qkgd', weights, values_split, preferred_element_typ...  7.24 us
  transfers between devices with their start and end apart: 3, of which 3 were waited for; matrix products, arithmetic and copies ran while one was open for 6% of the time, Pallas kernels for 0%

commit v1 on v0

--- a/solution.py
+++ b/solution.py
@@ -1,6 +1,11 @@
+import functools
+
 import jax
 import jax.numpy as jnp
+import numpy as np
 from jax import lax
+from jax.experimental import pallas as pl
+from jax.experimental.pallas import tpu as pltpu
 from jax.sharding import PartitionSpec as P
 
 EPS = 1e-06
@@ -71,7 +76,7 @@
     return mixture.astype(jnp.bfloat16).reshape(slot_len, query_width)
 
 
-def on_device(
+def on_device_ops(
     hidden, lengths, dealing, norm_gain, w_query, w_key, w_value, query_gain, key_gain, w_out
 ):
     devices = lax.axis_size("req")
@@ -84,7 +89,9 @@
     capacity = slot_len // devices
     prompt_total = lengths.shape[0]
     prompt_ids = jnp.arange(prompt_total, dtype=jnp.int32)
-    prompt_ends = jnp.cumsum(lengths)
+    prompt_ends = jnp.sum(
+        jnp.where(prompt_ids[:, None] <= prompt_ids[None, :], lengths[:, None], 0), axis=0
+    )
     starts = prompt_ends - lengths
     packed_ids = jnp.arange(tok_rows, dtype=jnp.int32) * devices + home_index
     segment = jnp.sum((packed_ids[:, None] >= prompt_ends[None, :]).astype(jnp.int32), axis=1)
@@ -137,6 +144,321 @@
     return (hidden_out, kv_cache)
 
 
+STAGES = 4
+F32 = jnp.float32
+BF16 = jnp.bfloat16
+MESH = pl.DeviceIdType.MESH
+
+
+def flip(index, mask):
+    flipped = index
+    bit = 1
+    while bit <= mask:
+        if mask & bit:
+            flipped = flipped + bit * (1 - 2 * ((index // bit) % 2))
+        bit *= 2
+    return flipped
+
+
+def pick(which, choices):
+    total = jnp.zeros_like(which)
+    for place, choice in enumerate(choices):
+        total = total + jnp.where(which == place, choice, 0)
+    return total
+
+
+def whole_kernel(
+    n, len_ref, deal_ref, hid_ref, gain_ref, qg_ref, kg_ref, cos_ref, sin_ref,
+    wq_hbm, wk_hbm, wv_hbm, wo_hbm, out_ref, kv_ref,
+    wq, wk, wv, wo, snd, arr, xs, sb, ret, att,
+    w_sem, d_send, d_recv, f_send, f_recv, r_send, r_recv, a_send, a_recv,
+):
+    me = lax.axis_index("req")
+    t = lax.axis_index("tp")
+    yp = flip(t, 2)
+    sib = flip(t, 1)
+    tok = hid_ref.shape[0]
+    width = wq.shape[1]
+    head = qg_ref.shape[1]
+    q_heads = width // head
+    kv_heads = wk.shape[1] // head
+    group = q_heads // kv_heads
+    part = xs.shape[3]
+    parts = xs.shape[1]
+    run = arr.shape[2]
+    block = n * run
+
+    weight_copies = [
+        pltpu.make_async_copy(source, target, w_sem.at[k])
+        for k, (source, target) in enumerate(
+            ((wq_hbm, wq), (wk_hbm, wk), (wv_hbm, wv), (wo_hbm, wo))
+        )
+    ]
+    for copy in weight_copies:
+        copy.start()
+
+    barrier = pltpu.get_barrier_semaphore()
+    for o in range(1, n):
+        pl.semaphore_signal(barrier, inc=1, device_id={"req": flip(me, o)}, device_id_type=MESH)
+    for peer in (yp, sib):
+        pl.semaphore_signal(barrier, inc=1, device_id={"tp": peer}, device_id_type=MESH)
+
+    prompts = len_ref.shape[0]
+    lens = [len_ref[p] for p in range(prompts)]
+    starts = [jnp.int32(0)]
+    for p in range(prompts - 1):
+        starts.append(starts[-1] + lens[p])
+    dealt = [deal_ref[j] for j in range(n)]
+    d_start = [pick(d, starts) for d in dealt]
+    d_len = [pick(d, lens) for d in dealt]
+    first = [lax.rem(me - s + n * tok, n) for s in d_start]
+    base = [lax.div(s + f - me, n) for s, f in zip(d_start, first)]
+    my_start = pick(me, d_start)
+    my_len = pick(me, d_len)
+
+    def chosen(index, stage, rows):
+        source = index // run
+        step = index % run + stage * run
+        return (rows == pick(source, base) + step) & (
+            pick(source, first) + n * step < pick(source, d_len)
+        )
+
+    col = lax.broadcasted_iota(jnp.int32, (block, 1), 0)
+    row = lax.broadcasted_iota(jnp.int32, (1, block), 1)
+    tok_row = lax.broadcasted_iota(jnp.int32, (1, tok), 1)
+    tok_col = lax.broadcasted_iota(jnp.int32, (tok, 1), 0)
+
+    def place(index):
+        return n * (index % run) + lax.rem(index // run - my_start + n * tok, n)
+
+    to_slot = jnp.where(col == place(row), 1.0, 0.0).astype(BF16)
+    to_source = jnp.where(place(col) == row, 1.0, 0.0).astype(BF16)
+
+    own = pl.ds(pl.multiple_of(t * part, part), part)
+    hid = hid_ref[...].astype(F32)
+    inv = lax.rsqrt(jnp.mean(hid * hid, axis=-1, keepdims=True) + EPS)
+    normed = (hid_ref[:, own].astype(F32) * inv * gain_ref[:, own].astype(F32)).astype(BF16)
+
+    def dispatch(i, o):
+        peer = flip(me, o)
+        return pltpu.make_async_remote_copy(
+            src_ref=snd.at[i, peer], dst_ref=arr.at[i, me],
+            send_sem=d_send.at[i, o], recv_sem=d_recv.at[i, o],
+            device_id={"req": peer}, device_id_type=MESH,
+        )
+
+    def giveback(i, o):
+        peer = flip(me, o)
+        return pltpu.make_async_remote_copy(
+            src_ref=sb.at[i, peer], dst_ref=ret.at[i, me],
+            send_sem=r_send.at[i, o], recv_sem=r_recv.at[i, o],
+            device_id={"req": peer}, device_id_type=MESH,
+        )
+
+    def spread(i, k):
+        which = yp if k == 2 else t
+        return pltpu.make_async_remote_copy(
+            src_ref=xs.at[i, which], dst_ref=xs.at[i, which],
+            send_sem=f_send.at[i, k], recv_sem=f_recv.at[i, k],
+            device_id={"tp": yp if k == 0 else sib}, device_id_type=MESH,
+        )
+
+    def share(k):
+        which = yp if k == 2 else t
+        return pltpu.make_async_remote_copy(
+            src_ref=att.at[which], dst_ref=att.at[which],
+            send_sem=a_send.at[k], recv_sem=a_recv.at[k],
+            device_id={"tp": yp if k == 0 else sib}, device_id_type=MESH,
+        )
+
+    order = sorted(range(1, n), key=lambda o: (-(o // 2), o))
+    for i in range(STAGES):
+        select = jnp.where(chosen(col, i, tok_row), 1.0, 0.0).astype(BF16)
+        rows = jnp.dot(select, normed, preferred_element_type=F32).astype(BF16)
+        snd[i] = rows.reshape(n, run, part)
+        if i == 0:
+            pl.semaphore_wait(barrier, n + 1)
+        for o in order:
+            dispatch(i, o).start()
+
+    def first_hop(i):
+        arr[i, me] = snd[i, me]
+        for o in order:
+            dispatch(i, o).wait_recv()
+        xs[i, t] = jnp.dot(
+            to_slot, arr[i].reshape(block, part), preferred_element_type=F32
+        ).astype(BF16)
+        spread(i, 0).start()
+        spread(i, 1).start()
+
+    def second_hop(i):
+        spread(i, 0).wait_recv()
+        spread(i, 2).start()
+
+    def turn(values, gain, i):
+        rows = slice(i * block, (i + 1) * block)
+        scaled = values * lax.rsqrt(jnp.mean(values * values, axis=-1, keepdims=True) + EPS)
+        scaled = scaled * gain
+        swapped = pltpu.roll(scaled, head // 2, 1)
+        return (scaled * cos_ref[rows, :] + swapped * sin_ref[rows, :]).astype(BF16)
+
+    def project_stage(weights, i):
+        total = jnp.dot(xs[i, 0], weights[:part, :], preferred_element_type=F32)
+        for q in range(1, parts):
+            total += jnp.dot(
+                xs[i, q], weights[q * part : (q + 1) * part, :], preferred_element_type=F32
+            )
+        return total
+
+    def compute(i):
+        spread(i, 1).wait_recv()
+        spread(i, 2).wait_recv()
+        rows = slice(i * block, (i + 1) * block)
+        extent = (i + 1) * block
+        query_gain = qg_ref[...].astype(F32)
+        key_gain = kg_ref[...].astype(F32)
+        query = project_stage(wq, i)
+        key = project_stage(wk, i)
+        kv_ref[1, 0, rows, :] = project_stage(wv, i).astype(BF16)
+        for g in range(kv_heads):
+            lanes = slice(g * head, (g + 1) * head)
+            kv_ref[0, 0, rows, lanes] = turn(key[:, lanes], key_gain, i)
+        q_pos = lax.broadcasted_iota(jnp.int32, (block, extent), 0) + i * block
+        k_pos = lax.broadcasted_iota(jnp.int32, (block, extent), 1)
+        allowed = (k_pos <= q_pos) & (k_pos < my_len)
+        mixed = []
+        for h in range(q_heads):
+            lanes = slice(h // group * head, (h // group + 1) * head)
+            turned = turn(query[:, h * head : (h + 1) * head], query_gain, i)
+            scores = lax.dot_general(
+                turned, kv_ref[0, 0, :extent, lanes], (((1,), (1,)), ((), ())),
+                preferred_element_type=F32,
+            ) * head ** (-0.5)
+            scores = jnp.where(allowed, scores, -jnp.inf)
+            weights = jnp.exp(scores - jnp.max(scores, axis=-1, keepdims=True))
+            weights = weights * (1.0 / jnp.sum(weights, axis=-1, keepdims=True))
+            mixed.append(
+                jnp.dot(
+                    weights.astype(BF16), kv_ref[1, 0, :extent, lanes],
+                    preferred_element_type=F32,
+                ).astype(BF16)
+            )
+        back = jnp.dot(to_source, jnp.concatenate(mixed, axis=1), preferred_element_type=F32)
+        sb[i] = back.astype(BF16).reshape(n, run, width)
+        for o in order:
+            giveback(i, o).start()
+        ret[i, me] = sb[i, me]
+
+    first_hop(0)
+    second_hop(0)
+    for copy in weight_copies:
+        copy.wait()
+    for i in range(STAGES):
+        if i + 1 < STAGES:
+            first_hop(i + 1)
+        compute(i)
+        if i + 1 < STAGES:
+            second_hop(i + 1)
+
+    total = jnp.zeros((tok, width), F32)
+    for i in range(STAGES):
+        for o in order:
+            giveback(i, o).wait_recv()
+        select = jnp.where(chosen(row, i, tok_col), 1.0, 0.0).astype(BF16)
+        total += jnp.dot(select, ret[i].reshape(block, width), preferred_element_type=F32)
+    att[t] = total.astype(BF16)
+    share(0).start()
+    share(1).start()
+    share(0).wait_recv()
+    share(2).start()
+    share(1).wait_recv()
+    share(2).wait_recv()
+    summed = jnp.dot(att[0], wo[:width, :], preferred_element_type=F32)
+    for q in range(1, parts):
+        summed += jnp.dot(
+            att[q], wo[q * width : (q + 1) * width, :], preferred_element_type=F32
+        )
+    branch = summed.astype(BF16).astype(F32)
+    out_ref[...] = (hid_ref[:, own].astype(F32) + branch).astype(BF16)
+
+    for i in range(STAGES):
+        for o in order:
+            dispatch(i, o).wait_send()
+            giveback(i, o).wait_send()
+        for k in range(3):
+            spread(i, k).wait_send()
+    for k in range(3):
+        share(k).wait_send()
+
+
+def on_device(
+    hidden, lengths, dealing, norm_gain, w_query, w_key, w_value, query_gain, key_gain, w_out
+):
+    n = lax.axis_size("req")
+    parts = lax.axis_size("tp")
+    tok, features = hidden.shape
+    head = query_gain.shape[0]
+    width = w_query.shape[1]
+    kv_width = w_key.shape[1]
+    out_width = w_out.shape[1]
+    slot_len = 4 * tok
+    run = slot_len // n // STAGES
+    if n != 8 or parts != 4 or run % 16:
+        return on_device_ops(
+            hidden, lengths, dealing, norm_gain, w_query, w_key, w_value, query_gain, key_gain, w_out
+        )
+    half = head // 2
+    frequency = (THETA ** (-(np.arange(half) * 2.0) / head)).astype(np.float32)
+    angles = np.arange(slot_len, dtype=np.float32)[:, None] * frequency[None, :]
+    cosine = np.cos(angles.astype(np.float64)).astype(np.float32)
+    sine = np.sin(angles.astype(np.float64)).astype(np.float32)
+    cosines = jnp.asarray(np.concatenate([cosine, cosine], axis=1))
+    sines = jnp.asarray(np.concatenate([-sine, sine], axis=1))
+    part = features // parts
+    smem = pl.BlockSpec(memory_space=pltpu.SMEM)
+    vmem = pl.BlockSpec(memory_space=pltpu.VMEM)
+    hbm = pl.BlockSpec(memory_space=pl.ANY)
+    dma = pltpu.SemaphoreType.DMA
+    hidden_out, kv_cache = pl.pallas_call(
+        functools.partial(whole_kernel, n),
+        out_shape=(
+            jax.ShapeDtypeStruct((tok, out_width), BF16),
+            jax.ShapeDtypeStruct((2, 1, slot_len, kv_width), BF16),
+        ),
+        in_specs=[smem] * 2 + [vmem] * 6 + [hbm] * 4,
+        out_specs=(vmem, vmem),
+        scratch_shapes=[
+            pltpu.VMEM(w_query.shape, BF16),
+            pltpu.VMEM(w_key.shape, BF16),
+            pltpu.VMEM(w_value.shape, BF16),
+            pltpu.VMEM(w_out.shape, BF16),
+            pltpu.VMEM((STAGES, n, run, part), BF16),
+            pltpu.VMEM((STAGES, n, run, part), BF16),
+            pltpu.VMEM((STAGES, parts, n * run, part), BF16),
+            pltpu.VMEM((STAGES, n, run, width), BF16),
+            pltpu.VMEM((STAGES, n, run, width), BF16),
+            pltpu.VMEM((parts, tok, width), BF16),
+            dma((4,)),
+            dma((STAGES, n)),
+            dma((STAGES, n)),
+            dma((STAGES, 3)),
+            dma((STAGES, 3)),
+            dma((STAGES, n)),
+            dma((STAGES, n)),
+            dma((3,)),
+            dma((3,)),
+        ],
+        compiler_params=pltpu.CompilerParams(
+            collective_id=0, has_side_effects=True, vmem_limit_bytes=56 * 2**20
+        ),
+        name="attention_half",
+    )(
+        lengths, dealing, hidden, norm_gain.reshape(1, -1), query_gain.reshape(1, -1),
+        key_gain.reshape(1, -1), cosines, sines, w_query, w_key, w_value, w_out,
+    )
+    return hidden_out, kv_cache
+
+
 def solution(mesh):
     in_specs = (
         P("req", None),

time: 247 us -> 77 us (0.31)
  the two profiles are of different devices: /device:TPU:17 before, /device:TPU:1 now
where the time goes in v1:
time: 77 us; the launch traced here: 76.8 us
  Pallas kernels  70.9 us (92%)
  local copies, waits for them, and re-layouts  5.22 us (7%)
    pallas_call x1, Pallas kernels, on_device(): pl.pallas_call(functools.partial(whole_kernel, n), out_shape=(jax.ShapeDt...  70.9 us
    unnamed x2, local copies, waits for them, and re-layouts  3.93 us

profile of v1, /device:TPU:1, one launch (start us, length us, event | category | flops | bytes accessed | tf_op | source)
XLA Modules:
  0.0 76.8 jit_solution(16755453680713053754)
XLA Ops:
  0.6 1.3 %reshape.13.gain_ref = bf16[1,2048]{1,0:T(2,128)(2,1)} reshape(bf16[2048]{0:T(1024)(128)(2,1)} %param.15) | data formatting | bytes 8192 | tf_op jit(solution)/shard_map/reshape | solution.py:456
  1.9 70.9 %attention_half.1 = (bf16[256,512]{1,0:T(8,128)(2,1)}, bf16[2,1,1024,256]{3,2,1,0:T(8,128)(2,1)}) custom-call(s32[8]{0:T(128)} %len_ref.1, s32[8]{0:T(128)} %deal_ref.1, bf16[256,2048]{1,0:T(8,128)(2,1)} %hid_ref.1, bf16[1,2048]{1,0:T(2,128)(2,1)} %reshape.13.gain_ref, bf16[1,128]{1,0:T(2,128)(2,1)} %bitcast.2, bf16[1,128]{1,0:T(2,128)(2,1)} %bitcast.3, ...), custom_call_target="tpu_custom_call" | custom-call | tf_op jit(solution)/shard_map/attention_half/pallas_call | solution.py:422
  72.8 1.7 %copy.16 = bf16[256,512]{1,0:T(8,128)(2,1)} copy(bf16[256,512]{1,0:T(8,128)(2,1)} %get-tuple-element.4) | data formatting | bytes 524288
  74.5 2.3 %copy.17 = bf16[2,1,1024,256]{3,2,1,0:T(8,128)(2,1)} copy(bf16[2,1,1024,256]{3,2,1,0:T(8,128)(2,1)} %get-tuple-element.5) | data formatting | bytes 2097152

commit v2 on v0

--- a/solution.py
+++ b/solution.py
@@ -1,6 +1,11 @@
+import functools
+
 import jax
 import jax.numpy as jnp
+import numpy as np
 from jax import lax
+from jax.experimental import pallas as pl
+from jax.experimental.pallas import tpu as pltpu
 from jax.sharding import PartitionSpec as P
 
 EPS = 1e-06
@@ -71,7 +76,7 @@
     return mixture.astype(jnp.bfloat16).reshape(slot_len, query_width)
 
 
-def on_device(
+def on_device_ops(
     hidden, lengths, dealing, norm_gain, w_query, w_key, w_value, query_gain, key_gain, w_out
 ):
     devices = lax.axis_size("req")
@@ -84,7 +89,9 @@
     capacity = slot_len // devices
     prompt_total = lengths.shape[0]
     prompt_ids = jnp.arange(prompt_total, dtype=jnp.int32)
-    prompt_ends = jnp.cumsum(lengths)
+    prompt_ends = jnp.sum(
+        jnp.where(prompt_ids[:, None] <= prompt_ids[None, :], lengths[:, None], 0), axis=0
+    )
     starts = prompt_ends - lengths
     packed_ids = jnp.arange(tok_rows, dtype=jnp.int32) * devices + home_index
     segment = jnp.sum((packed_ids[:, None] >= prompt_ends[None, :]).astype(jnp.int32), axis=1)
@@ -137,6 +144,307 @@
     return (hidden_out, kv_cache)
 
 
+STAGES = 4
+F32 = jnp.float32
+BF16 = jnp.bfloat16
+MESH = pl.DeviceIdType.MESH
+
+
+def flip(index, mask):
+    flipped = index
+    bit = 1
+    while bit <= mask:
+        if mask & bit:
+            flipped = flipped + bit * (1 - 2 * ((index // bit) % 2))
+        bit *= 2
+    return flipped
+
+
+def pick(which, choices):
+    total = jnp.zeros_like(which)
+    for place, choice in enumerate(choices):
+        total = total + jnp.where(which == place, choice, 0)
+    return total
+
+
+def whole_kernel(
+    n, len_ref, deal_ref, hid_ref, gain_ref, qg_ref, kg_ref, table_ref,
+    wq_hbm, wk_hbm, wv_hbm, wo_hbm, out_ref, kv_ref,
+    wq, wk, wv, wo, kvb, scores, picked, att,
+    w_sem, m_send, m_recv, a_send, a_recv,
+):
+    me = lax.axis_index("req")
+    t = lax.axis_index("tp")
+    yp = flip(t, 2)
+    sib = flip(t, 1)
+    tok = hid_ref.shape[0]
+    width = wq.shape[1]
+    kv_width = wk.shape[1]
+    head = qg_ref.shape[1]
+    kv_heads = kv_width // head
+    group = width // head // kv_heads
+    out_width = out_ref.shape[1]
+    parts = att.shape[0]
+    piece = group * head
+    half = tok // 2
+    slot_len = table_ref.shape[0]
+    run = picked.shape[2]
+    block = n * run
+
+    weight_copies = [
+        pltpu.make_async_copy(source, target, w_sem.at[k])
+        for k, (source, target) in enumerate(
+            ((wk_hbm, wk), (wv_hbm, wv), (wq_hbm, wq), (wo_hbm, wo))
+        )
+    ]
+    for copy in weight_copies:
+        copy.start()
+
+    barrier = pltpu.get_barrier_semaphore()
+    far = (4, 6, 2)
+    for o in (1,) + far:
+        pl.semaphore_signal(barrier, inc=1, device_id={"req": flip(me, o)}, device_id_type=MESH)
+    for peer in (yp, sib):
+        pl.semaphore_signal(barrier, inc=1, device_id={"tp": peer}, device_id_type=MESH)
+
+    prompts = len_ref.shape[0]
+    lens = [len_ref[p] for p in range(prompts)]
+    starts = [jnp.int32(0)]
+    for p in range(prompts - 1):
+        starts.append(starts[-1] + lens[p])
+    mine = pick(me, [deal_ref[j] for j in range(n)])
+    my_start = pick(mine, starts)
+    my_len = pick(mine, lens)
+
+    row = lax.broadcasted_iota(jnp.int32, (1, tok), 1)
+    col = lax.broadcasted_iota(jnp.int32, (tok, 1), 0)
+    token = col * n + me
+    token_start = jnp.zeros_like(token)
+    for start in starts[1:]:
+        token_start = jnp.maximum(token_start, jnp.where(token >= start, start, 0))
+
+    slots = lax.broadcasted_iota(jnp.int32, (1, slot_len), 1)
+    at_position = jnp.where(token - token_start == slots, 1.0, 0.0).astype(BF16)
+    terms = jnp.dot(at_position, table_ref[...], preferred_element_type=F32)
+    turns = terms[:, : 2 * head] + terms[:, 2 * head : 4 * head] + terms[:, 4 * head :]
+    cosines, sines = turns[:, :head], turns[:, head:]
+
+    hid = hid_ref[...].astype(F32)
+    inv = lax.rsqrt(jnp.mean(hid * hid, axis=-1, keepdims=True) + EPS)
+    normed = (hid * inv * gain_ref[...].astype(F32)).astype(BF16)
+
+    def turn(values, gain):
+        scaled = values * lax.rsqrt(jnp.mean(values * values, axis=-1, keepdims=True) + EPS)
+        scaled = scaled * gain
+        return (scaled * cosines + pltpu.roll(scaled, head // 2, 1) * sines).astype(BF16)
+
+    def move(o, h, onward):
+        source = flip(me, o) if onward else me
+        rows = pl.ds(h * half, half)
+        slot = o + 1 if onward else o
+        return pltpu.make_async_remote_copy(
+            src_ref=kvb.at[source, rows], dst_ref=kvb.at[source, rows],
+            send_sem=m_send.at[slot, h], recv_sem=m_recv.at[slot, h],
+            device_id={"req": flip(me, 1 if onward else o)}, device_id_type=MESH,
+        )
+
+    def share(k, g):
+        which = yp if k == 2 else t
+        return pltpu.make_async_remote_copy(
+            src_ref=att.at[which, g], dst_ref=att.at[which, g],
+            send_sem=a_send.at[k, g], recv_sem=a_recv.at[k, g],
+            device_id={"tp": yp if k == 0 else sib}, device_id_type=MESH,
+        )
+
+    weight_copies[0].wait()
+    weight_copies[1].wait()
+    key = jnp.dot(normed, wk[...], preferred_element_type=F32)
+    value = jnp.dot(normed, wv[...], preferred_element_type=F32)
+    key_gain = kg_ref[...].astype(F32)
+    for g in range(kv_heads):
+        lanes = slice(g * head, (g + 1) * head)
+        kvb[me, :, lanes] = turn(key[:, lanes], key_gain)
+    kvb[me, :, kv_width:] = value.astype(BF16)
+    pl.semaphore_wait(barrier, 6)
+    for h in range(2):
+        for o in far:
+            move(o, h, False).start()
+        move(0, h, True).start()
+
+    weight_copies[2].wait()
+    query = jnp.dot(normed, wq[...], preferred_element_type=F32)
+    query_gain = qg_ref[...].astype(F32)
+    queries = [
+        turn(query[:, h * head : (h + 1) * head], query_gain) for h in range(width // head)
+    ]
+
+    def onward(o, h):
+        move(o, h, False).wait_recv()
+        move(o, h, True).start()
+
+    def wait_for(o):
+        for h in range(2):
+            move(o - 1, h, True).wait_recv()
+
+    def meet(o):
+        source = flip(me, o)
+        key_token = row * n + source
+        allowed = (key_token <= token) & (key_token >= token_start)
+        for h in range(width // head):
+            g = h // group
+            product = lax.dot_general(
+                queries[h], kvb[source, :, g * head : (g + 1) * head],
+                (((1,), (1,)), ((), ())), preferred_element_type=F32,
+            )
+            scores[h, :, o * tok : (o + 1) * tok] = jnp.where(
+                allowed, product * head ** (-0.5), -jnp.inf
+            )
+        first = lax.rem(source - my_start + n * tok, n)
+        begin = lax.div(my_start + first - source, n)
+        step = lax.broadcasted_iota(jnp.int32, (slot_len // n, 1), 0)
+        select = (row == begin + step) & (first + n * step < my_len)
+        rows = jnp.dot(
+            jnp.where(select, 1.0, 0.0).astype(BF16), kvb[source], preferred_element_type=F32
+        ).astype(BF16)
+        for i in range(STAGES):
+            picked[i, source] = rows[i * run : (i + 1) * run]
+
+    onward(2, 0)
+    onward(2, 1)
+    meet(0)
+    onward(4, 0)
+    onward(6, 0)
+    wait_for(1)
+    meet(1)
+    meet(2)
+    onward(4, 1)
+    onward(6, 1)
+    meet(4)
+    meet(6)
+    for o in (3, 5, 7):
+        wait_for(o)
+        meet(o)
+
+    for g in range(kv_heads):
+        for k in range(group):
+            h = g * group + k
+            whole = scores[h]
+            weights = jnp.exp(whole - jnp.max(whole, axis=-1, keepdims=True))
+            weights = weights * (1.0 / jnp.sum(weights, axis=-1, keepdims=True))
+            weights = weights.astype(BF16)
+            lanes = slice(kv_width + g * head, kv_width + (g + 1) * head)
+            mixed = jnp.zeros((tok, head), F32)
+            for o in range(n):
+                mixed += jnp.dot(
+                    weights[:, o * tok : (o + 1) * tok], kvb[flip(me, o), :, lanes],
+                    preferred_element_type=F32,
+                )
+            att[t, g, :, k * head : (k + 1) * head] = mixed.astype(BF16)
+        share(0, g).start()
+        share(1, g).start()
+
+    share(0, 0).wait_recv()
+    share(2, 0).start()
+
+    place = n * (row % run) + lax.rem(row // run - my_start + n * tok, n)
+    to_slot = jnp.where(col == place, 1.0, 0.0).astype(BF16)
+    for i in range(STAGES):
+        rows = jnp.dot(
+            to_slot, picked[i].reshape(block, 2 * kv_width), preferred_element_type=F32
+        ).astype(BF16)
+        kv_ref[0, 0, i * block : (i + 1) * block, :] = rows[:, :kv_width]
+        kv_ref[1, 0, i * block : (i + 1) * block, :] = rows[:, kv_width:]
+
+    share(0, 1).wait_recv()
+    share(2, 1).start()
+    weight_copies[3].wait()
+    for g in range(kv_heads):
+        share(1, g).wait_recv()
+        share(2, g).wait_recv()
+    summed = jnp.zeros((tok, out_width), F32)
+    for q in range(parts):
+        for g in range(kv_heads):
+            begin = q * width + g * piece
+            summed += jnp.dot(att[q, g], wo[begin : begin + piece, :], preferred_element_type=F32)
+    own = pl.ds(pl.multiple_of(t * out_width, out_width), out_width)
+    branch = summed.astype(BF16).astype(F32)
+    out_ref[...] = (hid_ref[:, own].astype(F32) + branch).astype(BF16)
+
+    for h in range(2):
+        for o in far:
+            move(o, h, False).wait_send()
+        for o in (0, 2, 4, 6):
+            move(o, h, True).wait_send()
+    for g in range(kv_heads):
+        for k in range(3):
+            share(k, g).wait_send()
+
+
+def on_device(
+    hidden, lengths, dealing, norm_gain, w_query, w_key, w_value, query_gain, key_gain, w_out
+):
+    n = lax.axis_size("req")
+    parts = lax.axis_size("tp")
+    tok, features = hidden.shape
+    head = query_gain.shape[0]
+    width = w_query.shape[1]
+    kv_width = w_key.shape[1]
+    out_width = w_out.shape[1]
+    slot_len = 4 * tok
+    run = slot_len // n // STAGES
+    if n != 8 or parts != 4 or run % 16 or n * run != tok:
+        return on_device_ops(
+            hidden, lengths, dealing, norm_gain, w_query, w_key, w_value, query_gain, key_gain, w_out
+        )
+    half = head // 2
+    frequency = (THETA ** (-(np.arange(half) * 2.0) / head)).astype(np.float32)
+    angles = np.arange(slot_len, dtype=np.float32)[:, None] * frequency[None, :]
+    cosine = np.cos(angles.astype(np.float64)).astype(np.float32)
+    sine = np.sin(angles.astype(np.float64)).astype(np.float32)
+    exact = np.concatenate([cosine, cosine, -sine, sine], axis=1)
+    terms = []
+    for _ in range(3):
+        terms.append(exact.astype(jnp.bfloat16))
+        exact = exact - terms[-1].astype(np.float32)
+    table = jnp.asarray(np.concatenate(terms, axis=1))
+    smem = pl.BlockSpec(memory_space=pltpu.SMEM)
+    vmem = pl.BlockSpec(memory_space=pltpu.VMEM)
+    hbm = pl.BlockSpec(memory_space=pl.ANY)
+    dma = pltpu.SemaphoreType.DMA
+    hidden_out, kv_cache = pl.pallas_call(
+        functools.partial(whole_kernel, n),
+        out_shape=(
+            jax.ShapeDtypeStruct((tok, out_width), BF16),
+            jax.ShapeDtypeStruct((2, 1, slot_len, kv_width), BF16),
+        ),
+        in_specs=[smem] * 2 + [vmem] * 5 + [hbm] * 4,
+        out_specs=(vmem, vmem),
+        scratch_shapes=[
+            pltpu.VMEM(w_query.shape, BF16),
+            pltpu.VMEM(w_key.shape, BF16),
+            pltpu.VMEM(w_value.shape, BF16),
+            pltpu.VMEM(w_out.shape, BF16),
+            pltpu.VMEM((n, tok, 2 * kv_width), BF16),
+            pltpu.VMEM((width // head, tok, n * tok), F32),
+            pltpu.VMEM((STAGES, n, run, 2 * kv_width), BF16),
+            pltpu.VMEM((parts, kv_width // head, tok, width * head // kv_width), BF16),
+            dma((4,)),
+            dma((n, 2)),
+            dma((n, 2)),
+            dma((3, kv_width // head)),
+            dma((3, kv_width // head)),
+        ],
+        compiler_params=pltpu.CompilerParams(
+            collective_id=0, has_side_effects=True, vmem_limit_bytes=56 * 2**20
+        ),
+        name="attention_half",
+    )(
+        lengths, dealing, hidden, norm_gain.reshape(1, -1), query_gain.reshape(1, -1),
+        key_gain.reshape(1, -1), table, w_query, w_key, w_value, w_out,
+    )
+    return hidden_out, kv_cache
+
+
 def solution(mesh):
     in_specs = (
         P("req", None),

time: 247 us -> 58.3 us (0.24)
  waiting for transfers between devices: 116 us -> 0 us
  Pallas kernels: 0 us -> 52.2 us
  matrix products: 32.3 us -> 0 us
  local copies, waits for them, and re-layouts: 36.7 us -> 5.22 us
  other arithmetic: 30.2 us -> 0 us
  between operations: 16.2 us -> 0.64 us
  starting transfers between devices: 13.5 us -> 0 us
    all_to_all x2 -> x0, waiting for transfers between devices: 99.2 us -> none  [the longest x1 77.7 us: on_device(): lax.all_to_all(jnp.where(send_valid[:, :, None], picked, jnp.zeros((), hi...]
    pallas_call x0 -> x1, Pallas kernels: none -> 52.2 us  [on_device(): pl.pallas_call(functools.partial(whole_kernel, n), out_shape=(jax.ShapeDt...]
    dot_general x5 -> x0, matrix products: 20.8 us -> none  [the longest x1 7.24 us: attend(): jnp.einsum('kgqs,skd->qkgd', weights, values_split, preferred_element_typ...]
    all_gather x1 -> x0, waiting for transfers between devices: 16.4 us -> none  [on_device(): lax.all_gather(attended, 'tp', axis=1, tiled=True)]
    all_to_all x2 -> x0, starting transfers between devices: 13.5 us -> none  [the longest x1 7.78 us: on_device(): lax.all_to_all(sendback, 'req', split_axis=1, concat_axis=1, tiled=True)]
    select_n x5 -> x0, other arithmetic: 11.7 us -> none  [the longest x1 10.2 us: on_device(): jnp.where(send_valid[:, :, None], picked, jnp.zeros((), hidden.dtype))]
    sub x1 -> x0, matrix products: 11.5 us -> none  [attend(): weights = jnp.exp(scores - row_max)]
    gather x2 -> x0, local copies, waits for them, and re-layouts: 11.3 us -> none  [the longest x1 10.2 us: on_device(): jnp.take(hidden, send_rows, axis=0)]
  transfers between devices with their start and end apart: 3 -> 0, of which waited for: 3 -> 0; matrix products, arithmetic and copies ran while one was open for 6% -> 0% of each run, Pallas kernels for 0% -> 0%
where the time goes in v2:
time: 58.3 us; the launch traced here: 58.1 us
  Pallas kernels  52.2 us (90%)
  local copies, waits for them, and re-layouts  5.22 us (9%)
  between operations  0.64 us (1%)
    pallas_call x1, Pallas kernels, on_device(): pl.pallas_call(functools.partial(whole_kernel, n), out_shape=(jax.ShapeDt...  52.2 us
    unnamed x2, local copies, waits for them, and re-layouts  3.93 us
    reshape x1, local copies, waits for them, and re-layouts, on_device(): norm_gain.reshape(1, -1)  1.29 us

profile of v2, /device:TPU:17, one launch (start us, length us, event | category | flops | bytes accessed | tf_op | source)
XLA Modules:
  0.0 58.1 jit_solution(11335107774124640021)
XLA Ops:
  0.6 1.3 %reshape.13.gain_ref = bf16[1,2048]{1,0:T(2,128)(2,1)} reshape(bf16[2048]{0:T(1024)(128)(2,1)} %param.14) | data formatting | bytes 8192 | tf_op jit(solution)/shard_map/reshape | solution.py:442
  1.9 52.2 %attention_half.1 = (bf16[256,512]{1,0:T(8,128)(2,1)}, bf16[2,1,1024,256]{3,2,1,0:T(8,128)(2,1)}) custom-call(s32[8]{0:T(128)} %len_ref.1, s32[8]{0:T(128)} %deal_ref.1, bf16[256,2048]{1,0:T(8,128)(2,1)} %hid_ref.1, bf16[1,2048]{1,0:T(2,128)(2,1)} %reshape.13.gain_ref, bf16[1,128]{1,0:T(2,128)(2,1)} %bitcast.2, bf16[1,128]{1,0:T(2,128)(2,1)} %bitcast.3, ...), custom_call_target="tpu_custom_call" | custom-call | tf_op jit(solution)/shard_map/attention_half/pallas_call | solution.py:414
  54.1 1.7 %copy.15 = bf16[256,512]{1,0:T(8,128)(2,1)} copy(bf16[256,512]{1,0:T(8,128)(2,1)} %get-tuple-element.4) | data formatting | bytes 524288
  55.8 2.3 %copy.16 = bf16[2,1,1024,256]{3,2,1,0:T(8,128)(2,1)} copy(bf16[2,1,1024,256]{3,2,1,0:T(8,128)(2,1)} %get-tuple-element.5) | data formatting | bytes 2097152

commit v3 on v2

--- a/solution.py
+++ b/solution.py
@@ -145,6 +145,7 @@
 
 
 STAGES = 4
+PIECES = 4
 F32 = jnp.float32
 BF16 = jnp.bfloat16
 MESH = pl.DeviceIdType.MESH
@@ -186,7 +187,7 @@
     out_width = out_ref.shape[1]
     parts = att.shape[0]
     piece = group * head
-    half = tok // 2
+    half = tok // PIECES
     slot_len = table_ref.shape[0]
     run = picked.shape[2]
     block = n * run
@@ -266,7 +267,7 @@
         kvb[me, :, lanes] = turn(key[:, lanes], key_gain)
     kvb[me, :, kv_width:] = value.astype(BF16)
     pl.semaphore_wait(barrier, 6)
-    for h in range(2):
+    for h in range(PIECES):
         for o in far:
             move(o, h, False).start()
         move(0, h, True).start()
@@ -283,7 +284,7 @@
         move(o, h, True).start()
 
     def wait_for(o):
-        for h in range(2):
+        for h in range(PIECES):
             move(o - 1, h, True).wait_recv()
 
     def meet(o):
@@ -309,16 +310,17 @@
         for i in range(STAGES):
             picked[i, source] = rows[i * run : (i + 1) * run]
 
-    onward(2, 0)
-    onward(2, 1)
+    for h in range(PIECES):
+        onward(2, h)
     meet(0)
-    onward(4, 0)
-    onward(6, 0)
-    wait_for(1)
-    meet(1)
-    meet(2)
-    onward(4, 1)
-    onward(6, 1)
+    for h in range(PIECES):
+        onward(4, h)
+        onward(6, h)
+        if h == 0:
+            wait_for(1)
+            meet(1)
+        if h == 1:
+            meet(2)
     meet(4)
     meet(6)
     for o in (3, 5, 7):
@@ -370,7 +372,7 @@
     branch = summed.astype(BF16).astype(F32)
     out_ref[...] = (hid_ref[:, own].astype(F32) + branch).astype(BF16)
 
-    for h in range(2):
+    for h in range(PIECES):
         for o in far:
             move(o, h, False).wait_send()
         for o in (0, 2, 4, 6):
@@ -429,8 +431,8 @@
             pltpu.VMEM((STAGES, n, run, 2 * kv_width), BF16),
             pltpu.VMEM((parts, kv_width // head, tok, width * head // kv_width), BF16),
             dma((4,)),
-            dma((n, 2)),
-            dma((n, 2)),
+            dma((n, PIECES)),
+            dma((n, PIECES)),
             dma((3, kv_width // head)),
             dma((3, kv_width // head)),
         ],

time: 58.3 us -> 57.2 us (0.981)
  Pallas kernels: 52.2 us -> 51.1 us
    pallas_call x1, Pallas kernels: 52.2 us -> 51.1 us  [on_device(): pl.pallas_call(functools.partial(whole_kernel, n), out_shape=(jax.ShapeDt...]
where the time goes in v3:
time: 57.2 us; the launch traced here: 56.9 us
  Pallas kernels  51.1 us (89%)
  local copies, waits for them, and re-layouts  5.22 us (9%)
  between operations  0.64 us (1%)
    pallas_call x1, Pallas kernels, on_device(): pl.pallas_call(functools.partial(whole_kernel, n), out_shape=(jax.ShapeDt...  51.1 us
    unnamed x2, local copies, waits for them, and re-layouts  3.93 us
    reshape x1, local copies, waits for them, and re-layouts, on_device(): norm_gain.reshape(1, -1)  1.29 us

profile of v3, /device:TPU:17, one launch (start us, length us, event | category | flops | bytes accessed | tf_op | source)
XLA Modules:
  0.0 56.9 jit_solution(15212865041416795161)
XLA Ops:
  0.6 1.3 %reshape.13.gain_ref = bf16[1,2048]{1,0:T(2,128)(2,1)} reshape(bf16[2048]{0:T(1024)(128)(2,1)} %param.14) | data formatting | bytes 8192 | tf_op jit(solution)/shard_map/reshape | solution.py:444
  1.9 51.1 %attention_half.1 = (bf16[256,512]{1,0:T(8,128)(2,1)}, bf16[2,1,1024,256]{3,2,1,0:T(8,128)(2,1)}) custom-call(s32[8]{0:T(128)} %len_ref.1, s32[8]{0:T(128)} %deal_ref.1, bf16[256,2048]{1,0:T(8,128)(2,1)} %hid_ref.1, bf16[1,2048]{1,0:T(2,128)(2,1)} %reshape.13.gain_ref, bf16[1,128]{1,0:T(2,128)(2,1)} %bitcast.2, bf16[1,128]{1,0:T(2,128)(2,1)} %bitcast.3, ...), custom_call_target="tpu_custom_call" | custom-call | tf_op jit(solution)/shard_map/attention_half/pallas_call | solution.py:416
  53.0 1.7 %copy.15 = bf16[256,512]{1,0:T(8,128)(2,1)} copy(bf16[256,512]{1,0:T(8,128)(2,1)} %get-tuple-element.4) | data formatting | bytes 524288
  54.7 2.3 %copy.16 = bf16[2,1,1024,256]{3,2,1,0:T(8,128)(2,1)} copy(bf16[2,1,1024,256]{3,2,1,0:T(8,128)(2,1)} %get-tuple-element.5) | data formatting | bytes 2097152

commit v4 on v3

--- a/solution.py
+++ b/solution.py
@@ -279,6 +279,8 @@
         turn(query[:, h * head : (h + 1) * head], query_gain) for h in range(width // head)
     ]
 
+    tops = [jnp.full((tok, 1), -jnp.inf, F32)] * len(queries)
+
     def onward(o, h):
         move(o, h, False).wait_recv()
         move(o, h, True).start()
@@ -297,9 +299,9 @@
                 queries[h], kvb[source, :, g * head : (g + 1) * head],
                 (((1,), (1,)), ((), ())), preferred_element_type=F32,
             )
-            scores[h, :, o * tok : (o + 1) * tok] = jnp.where(
-                allowed, product * head ** (-0.5), -jnp.inf
-            )
+            tile = jnp.where(allowed, product * head ** (-0.5), -jnp.inf)
+            scores[h, :, o * tok : (o + 1) * tok] = tile
+            tops[h] = jnp.maximum(tops[h], jnp.max(tile, axis=-1, keepdims=True))
         first = lax.rem(source - my_start + n * tok, n)
         begin = lax.div(my_start + first - source, n)
         step = lax.broadcasted_iota(jnp.int32, (slot_len // n, 1), 0)
@@ -330,8 +332,7 @@
     for g in range(kv_heads):
         for k in range(group):
             h = g * group + k
-            whole = scores[h]
-            weights = jnp.exp(whole - jnp.max(whole, axis=-1, keepdims=True))
+            weights = jnp.exp(scores[h] - tops[h])
             weights = weights * (1.0 / jnp.sum(weights, axis=-1, keepdims=True))
             weights = weights.astype(BF16)
             lanes = slice(kv_width + g * head, kv_width + (g + 1) * head)

time: 57.2 us -> 56.9 us (level)
  no operation moved by 1% of the time
where the time goes in v4:
time: 56.9 us; the launch traced here: 56.7 us
  Pallas kernels  50.8 us (89%)
  local copies, waits for them, and re-layouts  5.22 us (9%)
  between operations  0.64 us (1%)
    pallas_call x1, Pallas kernels, on_device(): pl.pallas_call(functools.partial(whole_kernel, n), out_shape=(jax.ShapeDt...  50.8 us
    unnamed x2, local copies, waits for them, and re-layouts  3.93 us
    reshape x1, local copies, waits for them, and re-layouts, on_device(): norm_gain.reshape(1, -1)  1.29 us

profile of v4, /device:TPU:17, one launch (start us, length us, event | category | flops | bytes accessed | tf_op | source)
XLA Modules:
  0.0 56.7 jit_solution(5146980479773132066)
XLA Ops:
  0.6 1.3 %reshape.13.gain_ref = bf16[1,2048]{1,0:T(2,128)(2,1)} reshape(bf16[2048]{0:T(1024)(128)(2,1)} %param.14) | data formatting | bytes 8192 | tf_op jit(solution)/shard_map/reshape | solution.py:445
  1.9 50.8 %attention_half.1 = (bf16[256,512]{1,0:T(8,128)(2,1)}, bf16[2,1,1024,256]{3,2,1,0:T(8,128)(2,1)}) custom-call(s32[8]{0:T(128)} %len_ref.1, s32[8]{0:T(128)} %deal_ref.1, bf16[256,2048]{1,0:T(8,128)(2,1)} %hid_ref.1, bf16[1,2048]{1,0:T(2,128)(2,1)} %reshape.13.gain_ref, bf16[1,128]{1,0:T(2,128)(2,1)} %bitcast.2, bf16[1,128]{1,0:T(2,128)(2,1)} %bitcast.3, ...), custom_call_target="tpu_custom_call" | custom-call | tf_op jit(solution)/shard_map/attention_half/pallas_call | solution.py:417
  52.7 1.7 %copy.15 = bf16[256,512]{1,0:T(8,128)(2,1)} copy(bf16[256,512]{1,0:T(8,128)(2,1)} %get-tuple-element.4) | data formatting | bytes 524288
  54.4 2.3 %copy.16 = bf16[2,1,1024,256]{3,2,1,0:T(8,128)(2,1)} copy(bf16[2,1,1024,256]{3,2,1,0:T(8,128)(2,1)} %get-tuple-element.5) | data formatting | bytes 2097152
